TPU v7x, 32 devices: a whole 2x2x4 slice. The times are simulated.
32 devices in a mesh: inner: 4 (over z), outer: 8 (over y, x, core).
Axes of the slice: x: 2, y: 2, z: 4, core: 2. Of those that a mesh axis runs over, the one named last changes fastest.
Arguments:
- features: bfloat16 [262144, 256], P(('inner', 'outer')), may hold values from -6 to 6
- tiles: bfloat16 [2048, 8, 128, 128], P(('inner', 'outer')), may hold values from -0.1875 to 0.1875
- tile_src: int32 [2048, 8], P(('inner', 'outer')), may hold values from 0 to 111, as said below
- tile_count: int32 [2048], P(('inner', 'outer')), may hold values from 1 to 8
- node_count: int32 [32], P(('inner', 'outer')), may hold values from 2730 to 8192
- boundary: int32 [32, 8], P(('inner', 'outer')), may hold values from 0 to 63, as said below
- send_inner: int32 [32, 4, 4], P(('inner', 'outer')), may hold values from 0 to 7
- count_inner: int32 [32, 4], P(('inner', 'outer')), may hold values from 0 to 4, as said below
- send_outer: int32 [32, 8, 4], P(('inner', 'outer')), may hold values from 0 to 7
- count_outer: int32 [32, 8], P(('inner', 'outer')), may hold values from 0 to 4, as said below
- w_first: bfloat16 [256, 256], replicated, may hold values from -0.375 to 0.375
- gamma: float32 [256], replicated, may hold values from 0.25 to 1.75
- beta: float32 [256], replicated, may hold values from -3 to 3
- w_second: bfloat16 [256, 256], replicated, may hold values from -0.375 to 0.375
- b_second: float32 [256], replicated, may hold values from -3 to 3
Outputs:
- updated: bfloat16 [262144, 256], P(('inner', 'outer'))
Inputs may be any that keep to these rules, and one draw needn't show every extreme that they name: `tile_src`: index into the partition's source table; a slot index that is read names a slot its sender fills. `boundary`: distinct block numbers within a partition. `count_inner`: zero toward the partition itself, at least one toward every other peer. `count_outer`: zero toward the partition itself, at least one toward every other peer.
All inputs are finite; a program needn't handle non-finite values.
Results may differ from a plain program's by a relative error of at most 0.0053.
Values may be sent and summed in bfloat16 or wider, within the bound.
A program may use at most 128 MiB of HBM per device.

v0:
```python
import math
import jax
import jax.numpy as jnp
from jax import lax
from jax.sharding import PartitionSpec as P

EPSILON = 1e-05


def packed(blocks, border, lists, counts, capacity):
    chosen = blocks[border[lists]]
    keep = jnp.arange(capacity)[None, :] < counts[:, None]
    return jnp.where(keep[:, :, None, None], chosen, jnp.zeros((), blocks.dtype))


def local(
    features,
    tiles,
    tile_src,
    tile_count,
    node_count,
    boundary,
    send_inner,
    count_inner,
    send_outer,
    count_outer,
    w_first,
    gamma,
    beta,
    w_second,
    b_second,
):
    node_dev, width = features.shape
    nblocks, per_block, block_rows = (tiles.shape[0], tiles.shape[1], tiles.shape[2])
    capacity = send_inner.shape[2]
    zero_bf = jnp.zeros((), jnp.bfloat16)
    filled = node_count[0]
    live = jnp.arange(node_dev) < filled
    features_live = jnp.where(live[:, None], features, zero_bf)
    blocks = features_live.reshape(nblocks, block_rows, width)
    border = boundary[0]
    from_inner = lax.all_to_all(
        packed(blocks, border, send_inner[0], count_inner[0], capacity),
        "inner",
        split_axis=0,
        concat_axis=0,
        tiled=True,
    )
    from_outer = lax.all_to_all(
        packed(blocks, border, send_outer[0], count_outer[0], capacity),
        "outer",
        split_axis=0,
        concat_axis=0,
        tiled=True,
    )
    table = jnp.concatenate(
        [
            blocks,
            from_inner.reshape(-1, block_rows, width),
            from_outer.reshape(-1, block_rows, width),
            jnp.zeros((1, block_rows, width), jnp.bfloat16),
        ],
        axis=0,
    )
    empty_slot = table.shape[0] - 1
    used = jnp.arange(per_block)[None, :] < tile_count[:, None]
    sources = jnp.where(used, tile_src, empty_slot)
    group = math.gcd(nblocks, 8)

    def aggregate(item):
        tile_group, source_group = item
        gathered = table[source_group]
        return jnp.einsum(
            "bjrk,bjkf->brf", tile_group, gathered, preferred_element_type=jnp.float32
        )

    summed = lax.map(
        aggregate,
        (
            tiles.reshape(-1, group, per_block, block_rows, block_rows),
            sources.reshape(-1, group, per_block),
        ),
    )
    combined = (features_live.astype(jnp.float32) + summed.reshape(node_dev, width)).astype(
        jnp.bfloat16
    )
    first = jnp.dot(combined, w_first, preferred_element_type=jnp.float32)
    count_local = filled.astype(jnp.float32).reshape(1)
    masked = jnp.where(live[:, None], first, 0.0)
    totals = lax.psum(
        (count_local, jnp.sum(masked, axis=0), jnp.sum(masked * masked, axis=0)), ("inner", "outer")
    )
    mean = totals[1] / totals[0]
    variance = totals[2] / totals[0] - mean * mean
    normed = jax.nn.relu(gamma * (first - mean) * lax.rsqrt(variance + EPSILON) + beta).astype(
        jnp.bfloat16
    )
    output = jnp.dot(normed, w_second, preferred_element_type=jnp.float32) + b_second
    return jnp.where(live[:, None], output, 0.0).astype(jnp.bfloat16)


def solution(mesh):
    in_specs = (
        P(("inner", "outer"), None),
        P(("inner", "outer"), None, None, None),
        P(("inner", "outer"), None),
        P(("inner", "outer")),
        P(("inner", "outer")),
        P(("inner", "outer"), None),
        P(("inner", "outer"), None, None),
        P(("inner", "outer"), None),
        P(("inner", "outer"), None, None),
        P(("inner", "outer"), None),
        P(),
        P(),
        P(),
        P(),
        P(),
    )
    out_specs = P(("inner", "outer"), None)
    return jax.shard_map(local, mesh=mesh, in_specs=in_specs, out_specs=out_specs, check_vma=False)
```

profile of v0, /device:TPU:12, one launch (start us, length us, event | category | flops | bytes accessed | tf_op | source)
XLA Modules:
  0.0 223.1 jit_solution(13318727625451619962)
XLA Ops:
  1.5 1.3 gather_fusion.1
  3.7 5.2 %broadcast_select_fusion = bf16[8192,256]{1,0:T(8,128)(2,1)} fusion(bf16[8192,256]{1,0:T(8,128)(2,1)} %param.17, pred[8192]{0:T(1024)(128)(4,1)S(1)} %iota_compare_fusion), kind=kLoop, calls=%fused_computation.27 | loop fusion | flops 2097152 | bytes 8396800 | tf_op jit(solution)/shard_map/jit(_where)/select_n | solution.py:39
  9.0 2.8 %gather_fusion.2 = bf16[16,128,256]{2,1,0:T(8,128)(2,1)S(1)} fusion(bf16[64,128,256]{2,1,0:T(8,128)(2,1)} %bitcast.65, s32[1024]{0:T(1024)S(1)} %pad_clamp_fusion.3), kind=kCustom, calls=%fused_computation.2 | custom fusion | bytes 2097216 | tf_op jit(solution)/shard_map/gather | solution.py:11
  11.8 1.1 broadcast_select_fusion.2
  12.9 5.3 %all-to-all-start = ((bf16[4,4,128,256]{3,2,1,0:T(8,128)(2,1)}), bf16[4,4,128,256]{3,2,1,0:T(8,128)(2,1)S(1)}, u32[]{:S(2)}, u32[]{:S(2)}) async-start(bf16[4,4,128,256]{3,2,1,0:T(8,128)(2,1)} %broadcast_select_fusion.2), calls=%async_computation | async-start | bytes 2097152 | tf_op jit(solution)/shard_map/all_to_all | solution.py:42
  19.5 2.9 %gather_fusion.4 = bf16[32,128,256]{2,1,0:T(8,128)(2,1)S(1)} fusion(bf16[64,128,256]{2,1,0:T(8,128)(2,1)} %bitcast.66, s32[1024]{0:T(1024)S(1)} %pad_clamp_fusion.1), kind=kCustom, calls=%fused_computation.4 | custom fusion | bytes 4194432 | tf_op jit(solution)/shard_map/gather | solution.py:11
  22.4 1.6 broadcast_select_fusion.1
  24.0 16.6 %all-to-all-done = bf16[4,4,128,256]{3,2,1,0:T(8,128)(2,1)S(1)} async-done(((bf16[4,4,128,256]{3,2,1,0:T(8,128)(2,1)}), bf16[4,4,128,256]{3,2,1,0:T(8,128)(2,1)S(1)}, u32[]{:S(2)}, u32[]{:S(2)}) %all-to-all-start) | async-done | bytes 1048608 | tf_op jit(solution)/shard_map/all_to_all | solution.py:42
  40.7 4.2 %all-to-all-start.1 = ((bf16[8,4,128,256]{3,2,1,0:T(8,128)(2,1)}), bf16[8,4,128,256]{3,2,1,0:T(8,128)(2,1)S(1)}, u32[]{:S(2)}, u32[]{:S(2)}) async-start(bf16[8,4,128,256]{3,2,1,0:T(8,128)(2,1)} %broadcast_select_fusion.1), calls=%async_computation.1 | async-start | bytes 4194304 | tf_op jit(solution)/shard_map/all_to_all | solution.py:49
  45.1 25.0 %all-to-all-done.1 = bf16[8,4,128,256]{3,2,1,0:T(8,128)(2,1)S(1)} async-done(((bf16[8,4,128,256]{3,2,1,0:T(8,128)(2,1)}), bf16[8,4,128,256]{3,2,1,0:T(8,128)(2,1)S(1)}, u32[]{:S(2)}, u32[]{:S(2)}) %all-to-all-start.1) | async-done | bytes 2097184 | tf_op jit(solution)/shard_map/all_to_all | solution.py:49
  70.1 6.0 %maximum_maximum_fusion = bf16[113,128,256]{2,1,0:T(8,128)(2,1)} fusion(bf16[32,128,256]{2,1,0:T(8,128)(2,1)S(1)} %bitcast.69, bf16[16,128,256]{2,1,0:T(8,128)(2,1)S(1)} %bitcast.71, bf16[64,128,256]{2,1,0:T(8,128)(2,1)} %bitcast.67, bf16[113]{0:T(256)(128)(2,1)S(1)} %pad.3.clone), kind=kLoop, calls=%fused_computation.21 | loop fusion | flops 11108352 | bytes 14745826 | tf_op jit(solution)/shard_map/concatenate | solution.py:56
  76.1 85.3 %while.10 = (s32[]{:T(128)}, f32[8,8,128,256]{3,2,1,0:T(8,128)}, bf16[8,8,8,128,128]{4,3,2,1,0:T(8,128)(2,1)}, s32[8,8,8]{2,1,0:T(8,128)S(1)}, bf16[113,128,256]{2,1,0:T(8,128)(2,1)}, /*index=5*/s32[]{:T(128)}) while((s32[]{:T(128)}, f32[8,8,128,256]{3,2,1,0:T(8,128)}, bf16[8,8,8,128,128]{4,3,2,1,0:T(8,128)(2,1)}, s32[8,8,8]{2,1,0:T(8,128)S(1)}, ...), condition=%wide.region_1.2_spmd, body=%wide.region_0.1_spmd.sunk | while | flops 536872128 | bytes 15735369 | solution.py:77
  76.2 5.9 %gather_fusion = bf16[64,128,256]{2,1,0:T(8,128)(2,1)} fusion(bf16[113,128,256]{2,1,0:T(8,128)(2,1)} %get-tuple-element.98, s32[1024]{0:T(1024)S(1)} %pad_clamp_fusion.6), kind=kCustom, calls=%fused_computation.clone.1 | custom fusion | bytes 8388864 | tf_op jit(solution)/shard_map/while/body/eval_jaxpr/gather | solution.py:72
  82.1 4.6 %fusion.29 = f32[8,8,128,256]{3,2,1,0:T(8,128)} fusion(f32[8,8,128,256]{3,2,1,0:T(8,128)} %get-tuple-element.89, s32[]{:T(128)} %get-tuple-element.88, bf16[8,8,128,256]{3,2,1,0:T(8,128)(2,1)} %bitcast.64, bf16[8,8,8,128,128]{4,3,2,1,0:T(8,128)(2,1)} %get-tuple-element.96), kind=kOutput, calls=%fused_computation.9.clone.1 | convolution fusion | flops 536870912 | bytes 7341056 | tf_op jit(solution)/shard_map/while/body/eval_jaxpr/bjrk,bjkf->brf/dot_general | solution.py:73
  86.8 5.9 %gather_fusion = bf16[64,128,256]{2,1,0:T(8,128)(2,1)} fusion(bf16[113,128,256]{2,1,0:T(8,128)(2,1)} %get-tuple-element.98, s32[1024]{0:T(1024)S(1)} %pad_clamp_fusion.6), kind=kCustom, calls=%fused_computation.clone.1 | custom fusion | bytes 8388864 | tf_op jit(solution)/shard_map/while/body/eval_jaxpr/gather | solution.py:72
  92.8 4.7 %fusion.29 = f32[8,8,128,256]{3,2,1,0:T(8,128)} fusion(f32[8,8,128,256]{3,2,1,0:T(8,128)} %get-tuple-element.89, s32[]{:T(128)} %get-tuple-element.88, bf16[8,8,128,256]{3,2,1,0:T(8,128)(2,1)} %bitcast.64, bf16[8,8,8,128,128]{4,3,2,1,0:T(8,128)(2,1)} %get-tuple-element.96), kind=kOutput, calls=%fused_computation.9.clone.1 | convolution fusion | flops 536870912 | bytes 7341056 | tf_op jit(solution)/shard_map/while/body/eval_jaxpr/bjrk,bjkf->brf/dot_general | solution.py:73
  97.5 5.9 %gather_fusion = bf16[64,128,256]{2,1,0:T(8,128)(2,1)} fusion(bf16[113,128,256]{2,1,0:T(8,128)(2,1)} %get-tuple-element.98, s32[1024]{0:T(1024)S(1)} %pad_clamp_fusion.6), kind=kCustom, calls=%fused_computation.clone.1 | custom fusion | bytes 8388864 | tf_op jit(solution)/shard_map/while/body/eval_jaxpr/gather | solution.py:72
  103.5 4.6 %fusion.29 = f32[8,8,128,256]{3,2,1,0:T(8,128)} fusion(f32[8,8,128,256]{3,2,1,0:T(8,128)} %get-tuple-element.89, s32[]{:T(128)} %get-tuple-element.88, bf16[8,8,128,256]{3,2,1,0:T(8,128)(2,1)} %bitcast.64, bf16[8,8,8,128,128]{4,3,2,1,0:T(8,128)(2,1)} %get-tuple-element.96), kind=kOutput, calls=%fused_computation.9.clone.1 | convolution fusion | flops 536870912 | bytes 7341056 | tf_op jit(solution)/shard_map/while/body/eval_jaxpr/bjrk,bjkf->brf/dot_general | solution.py:73
  108.2 5.9 %gather_fusion = bf16[64,128,256]{2,1,0:T(8,128)(2,1)} fusion(bf16[113,128,256]{2,1,0:T(8,128)(2,1)} %get-tuple-element.98, s32[1024]{0:T(1024)S(1)} %pad_clamp_fusion.6), kind=kCustom, calls=%fused_computation.clone.1 | custom fusion | bytes 8388864 | tf_op jit(solution)/shard_map/while/body/eval_jaxpr/gather | solution.py:72
  114.1 4.6 %fusion.29 = f32[8,8,128,256]{3,2,1,0:T(8,128)} fusion(f32[8,8,128,256]{3,2,1,0:T(8,128)} %get-tuple-element.89, s32[]{:T(128)} %get-tuple-element.88, bf16[8,8,128,256]{3,2,1,0:T(8,128)(2,1)} %bitcast.64, bf16[8,8,8,128,128]{4,3,2,1,0:T(8,128)(2,1)} %get-tuple-element.96), kind=kOutput, calls=%fused_computation.9.clone.1 | convolution fusion | flops 536870912 | bytes 7341056 | tf_op jit(solution)/shard_map/while/body/eval_jaxpr/bjrk,bjkf->brf/dot_general | solution.py:73
  118.9 5.9 %gather_fusion = bf16[64,128,256]{2,1,0:T(8,128)(2,1)} fusion(bf16[113,128,256]{2,1,0:T(8,128)(2,1)} %get-tuple-element.98, s32[1024]{0:T(1024)S(1)} %pad_clamp_fusion.6), kind=kCustom, calls=%fused_computation.clone.1 | custom fusion | bytes 8388864 | tf_op jit(solution)/shard_map/while/body/eval_jaxpr/gather | solution.py:72
  124.8 4.6 %fusion.29 = f32[8,8,128,256]{3,2,1,0:T(8,128)} fusion(f32[8,8,128,256]{3,2,1,0:T(8,128)} %get-tuple-element.89, s32[]{:T(128)} %get-tuple-element.88, bf16[8,8,128,256]{3,2,1,0:T(8,128)(2,1)} %bitcast.64, bf16[8,8,8,128,128]{4,3,2,1,0:T(8,128)(2,1)} %get-tuple-element.96), kind=kOutput, calls=%fused_computation.9.clone.1 | convolution fusion | flops 536870912 | bytes 7341056 | tf_op jit(solution)/shard_map/while/body/eval_jaxpr/bjrk,bjkf->brf/dot_general | solution.py:73
  129.5 5.9 %gather_fusion = bf16[64,128,256]{2,1,0:T(8,128)(2,1)} fusion(bf16[113,128,256]{2,1,0:T(8,128)(2,1)} %get-tuple-element.98, s32[1024]{0:T(1024)S(1)} %pad_clamp_fusion.6), kind=kCustom, calls=%fused_computation.clone.1 | custom fusion | bytes 8388864 | tf_op jit(solution)/shard_map/while/body/eval_jaxpr/gather | solution.py:72
  135.4 4.6 %fusion.29 = f32[8,8,128,256]{3,2,1,0:T(8,128)} fusion(f32[8,8,128,256]{3,2,1,0:T(8,128)} %get-tuple-element.89, s32[]{:T(128)} %get-tuple-element.88, bf16[8,8,128,256]{3,2,1,0:T(8,128)(2,1)} %bitcast.64, bf16[8,8,8,128,128]{4,3,2,1,0:T(8,128)(2,1)} %get-tuple-element.96), kind=kOutput, calls=%fused_computation.9.clone.1 | convolution fusion | flops 536870912 | bytes 7341056 | tf_op jit(solution)/shard_map/while/body/eval_jaxpr/bjrk,bjkf->brf/dot_general | solution.py:73
  140.2 5.9 %gather_fusion = bf16[64,128,256]{2,1,0:T(8,128)(2,1)} fusion(bf16[113,128,256]{2,1,0:T(8,128)(2,1)} %get-tuple-element.98, s32[1024]{0:T(1024)S(1)} %pad_clamp_fusion.6), kind=kCustom, calls=%fused_computation.clone.1 | custom fusion | bytes 8388864 | tf_op jit(solution)/shard_map/while/body/eval_jaxpr/gather | solution.py:72
  146.1 4.6 %fusion.29 = f32[8,8,128,256]{3,2,1,0:T(8,128)} fusion(f32[8,8,128,256]{3,2,1,0:T(8,128)} %get-tuple-element.89, s32[]{:T(128)} %get-tuple-element.88, bf16[8,8,128,256]{3,2,1,0:T(8,128)(2,1)} %bitcast.64, bf16[8,8,8,128,128]{4,3,2,1,0:T(8,128)(2,1)} %get-tuple-element.96), kind=kOutput, calls=%fused_computation.9.clone.1 | convolution fusion | flops 536870912 | bytes 7341056 | tf_op jit(solution)/shard_map/while/body/eval_jaxpr/bjrk,bjkf->brf/dot_general | solution.py:73
  150.8 5.9 %gather_fusion = bf16[64,128,256]{2,1,0:T(8,128)(2,1)} fusion(bf16[113,128,256]{2,1,0:T(8,128)(2,1)} %get-tuple-element.98, s32[1024]{0:T(1024)S(1)} %pad_clamp_fusion.6), kind=kCustom, calls=%fused_computation.clone.1 | custom fusion | bytes 8388864 | tf_op jit(solution)/shard_map/while/body/eval_jaxpr/gather | solution.py:72
  156.8 4.7 %fusion.29 = f32[8,8,128,256]{3,2,1,0:T(8,128)} fusion(f32[8,8,128,256]{3,2,1,0:T(8,128)} %get-tuple-element.89, s32[]{:T(128)} %get-tuple-element.88, bf16[8,8,128,256]{3,2,1,0:T(8,128)(2,1)} %bitcast.64, bf16[8,8,8,128,128]{4,3,2,1,0:T(8,128)(2,1)} %get-tuple-element.96), kind=kOutput, calls=%fused_computation.9.clone.1 | convolution fusion | flops 536870912 | bytes 7341056 | tf_op jit(solution)/shard_map/while/body/eval_jaxpr/bjrk,bjkf->brf/dot_general | solution.py:73
  161.4 5.5 %fusion.12 = bf16[8192,256]{1,0:T(8,128)(2,1)S(1)} fusion(f32[8,8,128,256]{3,2,1,0:T(8,128)} %get-tuple-element.32, bf16[8192,256]{1,0:T(8,128)(2,1)} %param.17, pred[8192]{0:T(1024)(128)(4,1)S(1)} %iota_compare_fusion), kind=kLoop, calls=%fused_computation.17 | loop fusion | flops 8388608 | bytes 16785408 | tf_op jit(solution)/shard_map/convert_element_type | solution.py:84
  167.0 6.5 %multiply_reduce_fusion = (f32[256]{0:T(256)S(1)}, f32[256]{0:T(256)S(1)}, f32[8192,256]{1,0:T(8,128)}) fusion(pred[8192]{0:T(1024)(128)(4,1)S(1)} %iota_compare_fusion, bf16[8192,256]{1,0:T(8,128)(2,1)S(1)} %fusion.12, bf16[256,256]{1,0:T(8,128)(2,1)S(1)} %copy-done), kind=kOutput, calls=%fused_computation.19 | convolution fusion | flops 1082129920 | bytes 12724224 | tf_op jit(solution)/shard_map/dot_general | solution.py:87
  173.5 42.9 %all-reduce = (f32[256]{0:T(256)S(1)}, f32[]{:T(128)}, f32[256]{0:T(256)S(1)}) all-reduce(f32[256]{0:T(256)S(1)} %get-tuple-element.34, f32[]{:T(128)S(6)} %convert_element_type.17, f32[256]{0:T(256)S(1)} %get-tuple-element.33), channel_id=1, replica_groups=mesh['inner'=4,'outer'=8] {'inner','outer'}, use_global_device_ids=true, to_apply=%region_3.4 | all-reduce | flops 513 | bytes 4104 | tf_op jit(solution)/shard_map/psum | solution.py:90
  217.0 6.1 %fusion.11 = bf16[8192,256]{1,0:T(8,128)(2,1)} fusion(bf16[256,256]{1,0:T(8,128)(2,1)S(1)} %copy-done.5, f32[8192,256]{1,0:T(8,128)} %get-tuple-element.50, f32[256]{0:T(256)S(1)} %copy-done.6, f32[256]{0:T(256)S(1)} %copy-done.7, f32[256]{0:T(256)S(1)} %get-tuple-element.48, f32[256]{0:T(256)S(1)} %get-tuple-element.49, f32[256]{0:T(256)S(1)} %copy-done.8, ...), kind=kOutput, calls=%fused_computation.15 | convolution fusion | flops 1092616192 | bytes 12727296 | tf_op jit(solution)/shard_map/dot_general | solution.py:98
  (70 shorter events, 4.6 us)
Async XLA Ops:
  0.0 167.0 %copy-start = (bf16[256,256]{1,0:T(8,128)(2,1)S(1)}, bf16[256,256]{1,0:T(8,128)(2,1)}, u32[]{:S(2)}) copy-start(bf16[256,256]{1,0:T(8,128)(2,1)} %param.27) | copy-start | bytes 393220
  2.8 15.4 %copy-start.3 = (s32[1,8,4]{1,2,0:T(4,128)S(1)}, s32[1,8,4]{1,2,0:T(4,128)}, u32[]{:S(2)}) copy-start(s32[1,8,4]{1,2,0:T(4,128)} %param.25) | copy-start | bytes 388
  2.8 15.6 %copy-start.1 = (s32[1,8]{1,0:T(1,128)S(1)}, s32[1,8]{1,0:T(1,128)}, u32[]{:S(2)}) copy-start(s32[1,8]{1,0:T(1,128)} %param.22) | copy-start | bytes 100
  9.0 13.4 %copy-start.9 = (s32[1,8]{1,0:T(1,128)S(1)}, s32[1,8]{1,0:T(1,128)}, u32[]{:S(2)}) copy-start(s32[1,8]{1,0:T(1,128)} %param.26) | copy-start | bytes 100
  12.9 27.8 %all-to-all-start = ((bf16[4,4,128,256]{3,2,1,0:T(8,128)(2,1)}), bf16[4,4,128,256]{3,2,1,0:T(8,128)(2,1)S(1)}, u32[]{:S(2)}, u32[]{:S(2)}) async-start(bf16[4,4,128,256]{3,2,1,0:T(8,128)(2,1)} %broadcast_select_fusion.2), calls=%async_computation | async-start | bytes 2097152 | tf_op jit(solution)/shard_map/all_to_all | solution.py:42
  18.4 26.5 %copy-start.2 = (s32[64,8]{0,1:T(8,128)S(1)}, s32[64,8]{0,1:T(8,128)}, u32[]{:S(2)}) copy-start(s32[64,8]{0,1:T(8,128)} %param.19) | copy-start | bytes 6148
  18.4 26.5 %copy-start.4 = (s32[64]{0:T(128)S(1)}, s32[64]{0:T(128)}, u32[]{:S(2)}) copy-start(s32[64]{0:T(128)} %param.20) | copy-start | bytes 772
  40.7 29.4 %all-to-all-start.1 = ((bf16[8,4,128,256]{3,2,1,0:T(8,128)(2,1)}), bf16[8,4,128,256]{3,2,1,0:T(8,128)(2,1)S(1)}, u32[]{:S(2)}, u32[]{:S(2)}) async-start(bf16[8,4,128,256]{3,2,1,0:T(8,128)(2,1)} %broadcast_select_fusion.1), calls=%async_computation.1 | async-start | bytes 4194304 | tf_op jit(solution)/shard_map/all_to_all | solution.py:49
  167.0 50.0 %copy-start.5 = (bf16[256,256]{1,0:T(8,128)(2,1)S(1)}, bf16[256,256]{1,0:T(8,128)(2,1)}, u32[]{:S(2)}) copy-start(bf16[256,256]{1,0:T(8,128)(2,1)} %param.30) | copy-start | bytes 393220
  167.0 50.0 %copy-start.6 = (f32[256]{0:T(256)S(1)}, f32[256]{0:T(256)}, u32[]{:S(2)}) copy-start(f32[256]{0:T(256)} %param.31) | copy-start | bytes 3076
  167.0 50.0 %copy-start.7 = (f32[256]{0:T(256)S(1)}, f32[256]{0:T(256)}, u32[]{:S(2)}) copy-start(f32[256]{0:T(256)} %param.29) | copy-start | bytes 3076
  167.0 50.0 %copy-start.8 = (f32[256]{0:T(256)S(1)}, f32[256]{0:T(256)}, u32[]{:S(2)}) copy-start(f32[256]{0:T(256)} %param.28) | copy-start | bytes 3076
where the time goes:
time: 224 us; the launch traced here: 223 us
  local copies, waits for them, and re-layouts  56.8 us (25%)
  matrix products  49.6 us (22%)
  blocking collectives  42.9 us (19%)
  waiting for transfers between devices  41.6 us (19%)
  other arithmetic  21.8 us (10%)
  starting transfers between devices  9.54 us (4%)
    gather x8, local copies, waits for them, and re-layouts, aggregate(): gathered = table[source_group]  47.4 us
    psum x1, blocking collectives, local(): lax.psum((count_local, jnp.sum(masked, axis=0), jnp.sum(masked * masked,...  42.9 us
    dot_general x8, matrix products, aggregate(): jnp.einsum('bjrk,bjkf->brf', tile_group, gathered, preferred_element_type...  37.1 us
    all_to_all x1, waiting for transfers between devices, local(): lax.all_to_all(packed(blocks, border, send_outer[0], count_outer[0], capa...  25 us
    all_to_all x1, waiting for transfers between devices, local(): lax.all_to_all(packed(blocks, border, send_inner[0], count_inner[0], capa...  16.6 us
    gather x7, local copies, waits for them, and re-layouts, packed(): chosen = blocks[border[lists]]  7.94 us
    dot_general x1, matrix products, local(): first = jnp.dot(combined, w_first, preferred_element_type=jnp.float32)  6.45 us
    dot_general x1, matrix products, local(): jnp.dot(normed, w_second, preferred_element_type=jnp.float32) + b_second  6.09 us
  transfers between devices with their start and end apart: 2, of which 2 were waited for; matrix products, arithmetic and copies ran while one was open for 3% of the time, Pallas kernels for 0%

commit v1 on v0

--- a/solution.py
+++ b/solution.py
@@ -5,6 +5,18 @@
 from jax.sharding import PartitionSpec as P
 
 EPSILON = 1e-05
+
+
+def split_up(shard, dim, count):
+    dims = shard.shape
+    pieces = shard.reshape(*dims[:dim], count, dims[dim] // count, *dims[dim + 1 :])
+    return jnp.moveaxis(pieces, dim, 0)
+
+
+def laid_out(tiles, dim):
+    tiles = jnp.moveaxis(tiles, 0, dim)
+    dims = tiles.shape
+    return tiles.reshape(*dims[:dim], dims[dim] * dims[dim + 1], *dims[dim + 2 :])
 
 
 def packed(blocks, border, lists, counts, capacity):
@@ -46,13 +58,15 @@
         concat_axis=0,
         tiled=True,
     )
-    from_outer = lax.all_to_all(
-        packed(blocks, border, send_outer[0], count_outer[0], capacity),
-        "outer",
-        split_axis=0,
-        concat_axis=0,
-        tiled=True,
-    )
+    shard = packed(blocks, border, send_outer[0], count_outer[0], capacity)
+    size, position = (lax.axis_size("outer"), lax.axis_index("outer"))
+    blocks_2 = split_up(shard, 0, size)
+    gathered_2 = [blocks_2[position]]
+    for step in range(1, size):
+        sent = blocks_2[position ^ step]
+        gathered_2.append(lax.ppermute(sent, "outer", [(i, i ^ step) for i in range(size)]))
+    blocks_2 = jnp.stack(gathered_2)[position ^ jnp.arange(size)]
+    from_outer = laid_out(blocks_2, 0)
     table = jnp.concatenate(
         [
             blocks,

time: 224 us -> 211 us (0.942)
  waiting for transfers between devices: 41.6 us -> 10.3 us
  local copies, waits for them, and re-layouts: 56.8 us -> 68.5 us
  other arithmetic: 21.8 us -> 26.3 us
    all_to_all x1 -> x0, waiting for transfers between devices: 25 us -> none  [local(): lax.all_to_all(packed(blocks, border, send_outer[0], count_outer[0], capa...]
    all_to_all x1, waiting for transfers between devices: 16.6 us -> 2.69 us  [local(): lax.all_to_all(packed(blocks, border, send_inner[0], count_inner[0], capa...]
    ppermute x0 -> x7, waiting for transfers between devices: none -> 7.63 us  [local(): lax.ppermute(sent, 'outer', [(i, i ^ step) for i in range(size)])]
    unnamed x20 -> x33, local copies, waits for them, and re-layouts: 0.06 us -> 7.65 us
    ppermute x0 -> x7, starting transfers between devices: none -> 5.76 us  [local(): lax.ppermute(sent, 'outer', [(i, i ^ step) for i in range(size)])]
    select_n x8, other arithmetic: 0.03 us -> 5.44 us  [aggregate(): gathered = table[source_group]]
    all_to_all x1 -> x0, starting transfers between devices: 4.23 us -> none  [local(): lax.all_to_all(packed(blocks, border, send_outer[0], count_outer[0], capa...]
    gather x0 -> x1, local copies, waits for them, and re-layouts: none -> 2.27 us  [local(): blocks_2 = jnp.stack(gathered_2)[position ^ jnp.arange(size)]]
  transfers between devices with their start and end apart: 2 -> 8, of which waited for: 2 -> 3; matrix products, arithmetic and copies ran while one was open for 3% -> 6% of each run, Pallas kernels for 0% -> 0%
where the time goes in v1:
time: 211 us; the launch traced here: 210 us
  local copies, waits for them, and re-layouts  68.5 us (32%)
  matrix products  49.7 us (24%)
  blocking collectives  42.9 us (20%)
  other arithmetic  26.3 us (12%)
  starting transfers between devices  11.1 us (5%)
  waiting for transfers between devices  10.3 us (5%)
    gather x8, local copies, waits for them, and re-layouts, aggregate(): gathered = table[source_group]  47.4 us
    psum x1, blocking collectives, local(): lax.psum((count_local, jnp.sum(masked, axis=0), jnp.sum(masked * masked,...  42.9 us
    dot_general x8, matrix products, aggregate(): jnp.einsum('bjrk,bjkf->brf', tile_group, gathered, preferred_element_type...  37.1 us
    gather x7, local copies, waits for them, and re-layouts, packed(): chosen = blocks[border[lists]]  7.93 us
    unnamed x33, local copies, waits for them, and re-layouts  7.65 us
    ppermute x7, waiting for transfers between devices, local(): lax.ppermute(sent, 'outer', [(i, i ^ step) for i in range(size)])  7.63 us
    dot_general x1, matrix products, local(): first = jnp.dot(combined, w_first, preferred_element_type=jnp.float32)  6.48 us
    dot_general x1, matrix products, local(): jnp.dot(normed, w_second, preferred_element_type=jnp.float32) + b_second  6.09 us
  transfers between devices with their start and end apart: 8, of which 3 were waited for; matrix products, arithmetic and copies ran while one was open for 6% of the time, Pallas kernels for 0%

profile of v1, /device:TPU:12, one launch (start us, length us, event | category | flops | bytes accessed | tf_op | source)
XLA Modules:
  0.0 209.7 jit_solution(674657569201073170)
XLA Ops:
  4.3 5.2 %broadcast_select_fusion = bf16[8192,256]{1,0:T(8,128)(2,1)} fusion(bf16[8192,256]{1,0:T(8,128)(2,1)} %param.17, pred[8192]{0:T(1024)(128)(4,1)S(1)} %iota_compare_fusion), kind=kLoop, calls=%fused_computation.28 | loop fusion | flops 2097152 | bytes 8396800 | tf_op jit(solution)/shard_map/jit(_where)/select_n | solution.py:51
  9.6 2.9 %gather_fusion.4 = bf16[32,128,256]{2,1,0:T(8,128)(2,1)S(1)} fusion(bf16[64,128,256]{2,1,0:T(8,128)(2,1)} %bitcast.84, s32[1024]{0:T(1024)S(1)} %get-tuple-element.58), kind=kCustom, calls=%fused_computation.4 | custom fusion | bytes 4194432 | tf_op jit(solution)/shard_map/gather | solution.py:23
  15.3 1.5 collective-permute-start.1
  18.8 2.8 %gather_fusion.2 = bf16[16,128,256]{2,1,0:T(8,128)(2,1)S(1)} fusion(bf16[64,128,256]{2,1,0:T(8,128)(2,1)} %bitcast.85, s32[1024]{0:T(1024)S(1)} %get-tuple-element.59), kind=kCustom, calls=%fused_computation.2 | custom fusion | bytes 2097216 | tf_op jit(solution)/shard_map/gather | solution.py:23
  22.8 5.3 %all-to-all-start = ((bf16[4,4,128,256]{3,2,1,0:T(8,128)(2,1)}), bf16[4,4,128,256]{3,2,1,0:T(8,128)(2,1)S(1)}, u32[]{:S(2)}, u32[]{:S(2)}) async-start(bf16[4,4,128,256]{3,2,1,0:T(8,128)(2,1)} %broadcast_select_fusion.2), calls=%async_computation | async-start | bytes 2097152 | tf_op jit(solution)/shard_map/all_to_all | solution.py:54
  31.0 1.4 collective-permute-start.5
  37.3 4.1 %collective-permute-done.5 = bf16[1,4,128,256]{3,2,1,0:T(8,128)(2,1)S(1)} collective-permute-done((bf16[1,4,128,256]{3,2,1,0:T(8,128)(2,1)}, bf16[1,4,128,256]{3,2,1,0:T(8,128)(2,1)S(1)}, u32[]{:S(2)}, u32[]{:S(2)}) %collective-permute-start.5) | collective-permute-done | bytes 262176 | tf_op jit(solution)/shard_map/ppermute | solution.py:67
  41.4 3.5 %collective-permute-done.6 = bf16[1,4,128,256]{3,2,1,0:T(8,128)(2,1)S(1)} collective-permute-done((bf16[1,4,128,256]{3,2,1,0:T(8,128)(2,1)}, bf16[1,4,128,256]{3,2,1,0:T(8,128)(2,1)S(1)}, u32[]{:S(2)}, u32[]{:S(2)}) %collective-permute-start.6) | collective-permute-done | bytes 262176 | tf_op jit(solution)/shard_map/ppermute | solution.py:67
  46.3 2.3 %gather_fusion.5 = bf16[8,4,128,256]{3,2,1,0:T(8,128)(2,1)S(1)} fusion(bf16[8,4,128,256]{3,2,1,0:T(8,128)(2,1)} %bitcast.92, s32[1024]{0:T(1024)S(1)} %pad_clamp_fusion.1), kind=kCustom, calls=%fused_computation.5 | custom fusion | bytes 4194336 | tf_op jit(solution)/shard_map/gather | solution.py:68
  48.6 2.7 %all-to-all-done = bf16[4,4,128,256]{3,2,1,0:T(8,128)(2,1)S(1)} async-done(((bf16[4,4,128,256]{3,2,1,0:T(8,128)(2,1)}), bf16[4,4,128,256]{3,2,1,0:T(8,128)(2,1)S(1)}, u32[]{:S(2)}, u32[]{:S(2)}) %all-to-all-start) | async-done | bytes 1048608 | tf_op jit(solution)/shard_map/all_to_all | solution.py:54
  51.3 5.9 %maximum_maximum_fusion = bf16[113,128,256]{2,1,0:T(8,128)(2,1)} fusion(bf16[32,128,256]{2,1,0:T(8,128)(2,1)S(1)} %bitcast.88, bf16[16,128,256]{2,1,0:T(8,128)(2,1)S(1)} %bitcast.90, bf16[64,128,256]{2,1,0:T(8,128)(2,1)} %bitcast.86, bf16[113]{0:T(256)(128)(2,1)S(1)} %pad.3.clone), kind=kLoop, calls=%fused_computation.22 | loop fusion | flops 11108352 | bytes 14745826 | tf_op jit(solution)/shard_map/concatenate | solution.py:70
  57.2 90.7 %while.10 = (s32[]{:T(128)}, f32[8,8,128,256]{3,2,1,0:T(8,128)}, bf16[8,8,8,128,128]{4,3,2,1,0:T(8,128)(2,1)}, s32[8,8,8]{2,1,0:T(8,128)}, bf16[113,128,256]{2,1,0:T(8,128)(2,1)}, /*index=5*/s32[]{:T(128)}) while((s32[]{:T(128)}, f32[8,8,128,256]{3,2,1,0:T(8,128)}, bf16[8,8,8,128,128]{4,3,2,1,0:T(8,128)(2,1)}, s32[8,8,8]{2,1,0:T(8,128)}, ...), condition=%wide.region_1.2_spmd, body=%wide.region_0.1_spmd.sunk | while | flops 536872128 | bytes 15735369 | solution.py:91
  58.0 5.9 %gather_fusion = bf16[64,128,256]{2,1,0:T(8,128)(2,1)} fusion(bf16[113,128,256]{2,1,0:T(8,128)(2,1)} %get-tuple-element.107, s32[1024]{0:T(1024)S(1)} %pad_clamp_fusion.7), kind=kCustom, calls=%fused_computation.clone.1 | custom fusion | bytes 8388864 | tf_op jit(solution)/shard_map/while/body/eval_jaxpr/gather | solution.py:86
  63.9 4.6 %fusion.30 = f32[8,8,128,256]{3,2,1,0:T(8,128)} fusion(f32[8,8,128,256]{3,2,1,0:T(8,128)} %get-tuple-element.98, s32[]{:T(128)} %get-tuple-element.97, bf16[8,8,128,256]{3,2,1,0:T(8,128)(2,1)} %bitcast.83, bf16[8,8,8,128,128]{4,3,2,1,0:T(8,128)(2,1)} %get-tuple-element.105), kind=kOutput, calls=%fused_computation.10.clone.1 | convolution fusion | flops 536870912 | bytes 7341056 | tf_op jit(solution)/shard_map/while/body/eval_jaxpr/bjrk,bjkf->brf/dot_general | solution.py:87
  69.3 5.9 %gather_fusion = bf16[64,128,256]{2,1,0:T(8,128)(2,1)} fusion(bf16[113,128,256]{2,1,0:T(8,128)(2,1)} %get-tuple-element.107, s32[1024]{0:T(1024)S(1)} %pad_clamp_fusion.7), kind=kCustom, calls=%fused_computation.clone.1 | custom fusion | bytes 8388864 | tf_op jit(solution)/shard_map/while/body/eval_jaxpr/gather | solution.py:86
  75.3 4.6 %fusion.30 = f32[8,8,128,256]{3,2,1,0:T(8,128)} fusion(f32[8,8,128,256]{3,2,1,0:T(8,128)} %get-tuple-element.98, s32[]{:T(128)} %get-tuple-element.97, bf16[8,8,128,256]{3,2,1,0:T(8,128)(2,1)} %bitcast.83, bf16[8,8,8,128,128]{4,3,2,1,0:T(8,128)(2,1)} %get-tuple-element.105), kind=kOutput, calls=%fused_computation.10.clone.1 | convolution fusion | flops 536870912 | bytes 7341056 | tf_op jit(solution)/shard_map/while/body/eval_jaxpr/bjrk,bjkf->brf/dot_general | solution.py:87
  80.7 5.9 %gather_fusion = bf16[64,128,256]{2,1,0:T(8,128)(2,1)} fusion(bf16[113,128,256]{2,1,0:T(8,128)(2,1)} %get-tuple-element.107, s32[1024]{0:T(1024)S(1)} %pad_clamp_fusion.7), kind=kCustom, calls=%fused_computation.clone.1 | custom fusion | bytes 8388864 | tf_op jit(solution)/shard_map/while/body/eval_jaxpr/gather | solution.py:86
  86.6 4.6 %fusion.30 = f32[8,8,128,256]{3,2,1,0:T(8,128)} fusion(f32[8,8,128,256]{3,2,1,0:T(8,128)} %get-tuple-element.98, s32[]{:T(128)} %get-tuple-element.97, bf16[8,8,128,256]{3,2,1,0:T(8,128)(2,1)} %bitcast.83, bf16[8,8,8,128,128]{4,3,2,1,0:T(8,128)(2,1)} %get-tuple-element.105), kind=kOutput, calls=%fused_computation.10.clone.1 | convolution fusion | flops 536870912 | bytes 7341056 | tf_op jit(solution)/shard_map/while/body/eval_jaxpr/bjrk,bjkf->brf/dot_general | solution.py:87
  92.0 5.9 %gather_fusion = bf16[64,128,256]{2,1,0:T(8,128)(2,1)} fusion(bf16[113,128,256]{2,1,0:T(8,128)(2,1)} %get-tuple-element.107, s32[1024]{0:T(1024)S(1)} %pad_clamp_fusion.7), kind=kCustom, calls=%fused_computation.clone.1 | custom fusion | bytes 8388864 | tf_op jit(solution)/shard_map/while/body/eval_jaxpr/gather | solution.py:86
  97.9 4.6 %fusion.30 = f32[8,8,128,256]{3,2,1,0:T(8,128)} fusion(f32[8,8,128,256]{3,2,1,0:T(8,128)} %get-tuple-element.98, s32[]{:T(128)} %get-tuple-element.97, bf16[8,8,128,256]{3,2,1,0:T(8,128)(2,1)} %bitcast.83, bf16[8,8,8,128,128]{4,3,2,1,0:T(8,128)(2,1)} %get-tuple-element.105), kind=kOutput, calls=%fused_computation.10.clone.1 | convolution fusion | flops 536870912 | bytes 7341056 | tf_op jit(solution)/shard_map/while/body/eval_jaxpr/bjrk,bjkf->brf/dot_general | solution.py:87
  103.3 5.9 %gather_fusion = bf16[64,128,256]{2,1,0:T(8,128)(2,1)} fusion(bf16[113,128,256]{2,1,0:T(8,128)(2,1)} %get-tuple-element.107, s32[1024]{0:T(1024)S(1)} %pad_clamp_fusion.7), kind=kCustom, calls=%fused_computation.clone.1 | custom fusion | bytes 8388864 | tf_op jit(solution)/shard_map/while/body/eval_jaxpr/gather | solution.py:86
  109.3 4.6 %fusion.30 = f32[8,8,128,256]{3,2,1,0:T(8,128)} fusion(f32[8,8,128,256]{3,2,1,0:T(8,128)} %get-tuple-element.98, s32[]{:T(128)} %get-tuple-element.97, bf16[8,8,128,256]{3,2,1,0:T(8,128)(2,1)} %bitcast.83, bf16[8,8,8,128,128]{4,3,2,1,0:T(8,128)(2,1)} %get-tuple-element.105), kind=kOutput, calls=%fused_computation.10.clone.1 | convolution fusion | flops 536870912 | bytes 7341056 | tf_op jit(solution)/shard_map/while/body/eval_jaxpr/bjrk,bjkf->brf/dot_general | solution.py:87
  114.6 5.9 %gather_fusion = bf16[64,128,256]{2,1,0:T(8,128)(2,1)} fusion(bf16[113,128,256]{2,1,0:T(8,128)(2,1)} %get-tuple-element.107, s32[1024]{0:T(1024)S(1)} %pad_clamp_fusion.7), kind=kCustom, calls=%fused_computation.clone.1 | custom fusion | bytes 8388864 | tf_op jit(solution)/shard_map/while/body/eval_jaxpr/gather | solution.py:86
  120.6 4.7 %fusion.30 = f32[8,8,128,256]{3,2,1,0:T(8,128)} fusion(f32[8,8,128,256]{3,2,1,0:T(8,128)} %get-tuple-element.98, s32[]{:T(128)} %get-tuple-element.97, bf16[8,8,128,256]{3,2,1,0:T(8,128)(2,1)} %bitcast.83, bf16[8,8,8,128,128]{4,3,2,1,0:T(8,128)(2,1)} %get-tuple-element.105), kind=kOutput, calls=%fused_computation.10.clone.1 | convolution fusion | flops 536870912 | bytes 7341056 | tf_op jit(solution)/shard_map/while/body/eval_jaxpr/bjrk,bjkf->brf/dot_general | solution.py:87
  126.0 5.9 %gather_fusion = bf16[64,128,256]{2,1,0:T(8,128)(2,1)} fusion(bf16[113,128,256]{2,1,0:T(8,128)(2,1)} %get-tuple-element.107, s32[1024]{0:T(1024)S(1)} %pad_clamp_fusion.7), kind=kCustom, calls=%fused_computation.clone.1 | custom fusion | bytes 8388864 | tf_op jit(solution)/shard_map/while/body/eval_jaxpr/gather | solution.py:86
  131.9 4.6 %fusion.30 = f32[8,8,128,256]{3,2,1,0:T(8,128)} fusion(f32[8,8,128,256]{3,2,1,0:T(8,128)} %get-tuple-element.98, s32[]{:T(128)} %get-tuple-element.97, bf16[8,8,128,256]{3,2,1,0:T(8,128)(2,1)} %bitcast.83, bf16[8,8,8,128,128]{4,3,2,1,0:T(8,128)(2,1)} %get-tuple-element.105), kind=kOutput, calls=%fused_computation.10.clone.1 | convolution fusion | flops 536870912 | bytes 7341056 | tf_op jit(solution)/shard_map/while/body/eval_jaxpr/bjrk,bjkf->brf/dot_general | solution.py:87
  137.3 5.9 %gather_fusion = bf16[64,128,256]{2,1,0:T(8,128)(2,1)} fusion(bf16[113,128,256]{2,1,0:T(8,128)(2,1)} %get-tuple-element.107, s32[1024]{0:T(1024)S(1)} %pad_clamp_fusion.7), kind=kCustom, calls=%fused_computation.clone.1 | custom fusion | bytes 8388864 | tf_op jit(solution)/shard_map/while/body/eval_jaxpr/gather | solution.py:86
  143.3 4.7 %fusion.30 = f32[8,8,128,256]{3,2,1,0:T(8,128)} fusion(f32[8,8,128,256]{3,2,1,0:T(8,128)} %get-tuple-element.98, s32[]{:T(128)} %get-tuple-element.97, bf16[8,8,128,256]{3,2,1,0:T(8,128)(2,1)} %bitcast.83, bf16[8,8,8,128,128]{4,3,2,1,0:T(8,128)(2,1)} %get-tuple-element.105), kind=kOutput, calls=%fused_computation.10.clone.1 | convolution fusion | flops 536870912 | bytes 7341056 | tf_op jit(solution)/shard_map/while/body/eval_jaxpr/bjrk,bjkf->brf/dot_general | solution.py:87
  147.9 5.5 %fusion.12 = bf16[8192,256]{1,0:T(8,128)(2,1)S(1)} fusion(f32[8,8,128,256]{3,2,1,0:T(8,128)} %get-tuple-element.32, bf16[8192,256]{1,0:T(8,128)(2,1)} %param.17, pred[8192]{0:T(1024)(128)(4,1)S(1)} %iota_compare_fusion), kind=kLoop, calls=%fused_computation.18 | loop fusion | flops 8388608 | bytes 16785408 | tf_op jit(solution)/shard_map/convert_element_type | solution.py:98
  153.6 6.5 %multiply_reduce_fusion = (f32[256]{0:T(256)S(1)}, f32[256]{0:T(256)S(1)}, f32[8192,256]{1,0:T(8,128)}) fusion(pred[8192]{0:T(1024)(128)(4,1)S(1)} %iota_compare_fusion, bf16[8192,256]{1,0:T(8,128)(2,1)S(1)} %fusion.12, bf16[256,256]{1,0:T(8,128)(2,1)S(1)} %copy-done), kind=kOutput, calls=%fused_computation.20 | convolution fusion | flops 1082129920 | bytes 12724224 | tf_op jit(solution)/shard_map/dot_general | solution.py:101
  160.0 42.9 %all-reduce = (f32[256]{0:T(256)S(1)}, f32[]{:T(128)}, f32[256]{0:T(256)S(1)}) all-reduce(f32[256]{0:T(256)S(1)} %get-tuple-element.34, f32[]{:T(128)S(6)} %convert_element_type.17, f32[256]{0:T(256)S(1)} %get-tuple-element.33), channel_id=1, replica_groups=mesh['inner'=4,'outer'=8] {'inner','outer'}, use_global_device_ids=true, to_apply=%region_3.4 | all-reduce | flops 513 | bytes 4104 | tf_op jit(solution)/shard_map/psum | solution.py:104
  203.6 6.1 %fusion.11 = bf16[8192,256]{1,0:T(8,128)(2,1)} fusion(bf16[256,256]{1,0:T(8,128)(2,1)S(1)} %copy-done.7, f32[8192,256]{1,0:T(8,128)} %get-tuple-element.57, f32[256]{0:T(256)S(1)} %copy-done.8, f32[256]{0:T(256)S(1)} %copy-done.9, f32[256]{0:T(256)S(1)} %get-tuple-element.48, f32[256]{0:T(256)S(1)} %get-tuple-element.49, f32[256]{0:T(256)S(1)} %copy-done.10, ...), kind=kOutput, calls=%fused_computation.16 | convolution fusion | flops 1092616192 | bytes 12727296 | tf_op jit(solution)/shard_map/dot_general | solution.py:112
  (99 shorter events, 25.5 us)
Async XLA Ops:
  0.0 153.5 %copy-start = (bf16[256,256]{1,0:T(8,128)(2,1)S(1)}, bf16[256,256]{1,0:T(8,128)(2,1)}, u32[]{:S(2)}) copy-start(bf16[256,256]{1,0:T(8,128)(2,1)} %param.27) | copy-start | bytes 393220
  0.0 3.4 %copy-start.1 = (s32[1,8]{1,0:T(1,128)S(1)}, s32[1,8]{1,0:T(1,128)}, u32[]{:S(2)}) copy-start(s32[1,8]{1,0:T(1,128)} %param.22) | copy-start | bytes 100
  0.0 3.3 %copy-start.5 = (s32[1,4,4]{2,1,0:T(4,128)S(1)}, s32[1,4,4]{2,1,0:T(4,128)}, u32[]{:S(2)}) copy-start(s32[1,4,4]{2,1,0:T(4,128)} %param.23) | copy-start | bytes 196
  0.0 4.2 %copy-start.11 = (s32[1,8]{1,0:T(1,128)S(1)}, s32[1,8]{1,0:T(1,128)}, u32[]{:S(2)}) copy-start(s32[1,8]{1,0:T(1,128)} %param.26) | copy-start | bytes 100
  12.5 9.2 %copy-start.12 = (s32[1,4]{1,0:T(1,128)S(1)}, s32[1,4]{1,0:T(1,128)}, u32[]{:S(2)}) copy-start(s32[1,4]{1,0:T(1,128)} %param.24) | copy-start | bytes 52
  12.7 1.3 copy-start.2
  14.0 14.1 %copy-start.4 = (s32[64,8]{0,1:T(8,128)S(1)}, s32[64,8]{0,1:T(8,128)}, u32[]{:S(2)}) copy-start(s32[64,8]{0,1:T(8,128)} %param.19) | copy-start | bytes 6148
  14.0 14.1 %copy-start.6 = (s32[64]{0:T(128)S(1)}, s32[64]{0:T(128)}, u32[]{:S(2)}) copy-start(s32[64]{0:T(128)} %param.20) | copy-start | bytes 772
  15.3 15.7 %collective-permute-start = (bf16[1,4,128,256]{3,2,1,0:T(8,128)(2,1)}, bf16[1,4,128,256]{3,2,1,0:T(8,128)(2,1)}, u32[]{:S(2)}, u32[]{:S(2)}) collective-permute-start(bf16[1,4,128,256]{3,2,1,0:T(8,128)(2,1)} %get-tuple-element.56), channel_id=1, source_target_pairs={{0,1},{1,0},{2,3},{3,2},{4,5},{5,4},{6,7},{7,6},{8,9},{9,8},{10,11... | collective-permute-start | bytes 786440 | tf_op jit(solution)/shard_map/ppermute | solution.py:67
  15.3 18.1 %collective-permute-start.1 = (bf16[1,4,128,256]{3,2,1,0:T(8,128)(2,1)}, bf16[1,4,128,256]{3,2,1,0:T(8,128)(2,1)}, u32[]{:S(2)}, u32[]{:S(2)}) collective-permute-start(bf16[1,4,128,256]{3,2,1,0:T(8,128)(2,1)} %get-tuple-element.55), channel_id=1, source_target_pairs={{0,2},{1,3},{2,0},{3,1},{4,6},{5,7},{6,4},{7,5},{8,10},{9,11},{10,... | collective-permute-start | bytes 786440 | tf_op jit(solution)/shard_map/ppermute | solution.py:67
  16.8 18.4 %collective-permute-start.2 = (bf16[1,4,128,256]{3,2,1,0:T(8,128)(2,1)}, bf16[1,4,128,256]{3,2,1,0:T(8,128)(2,1)}, u32[]{:S(2)}, u32[]{:S(2)}) collective-permute-start(bf16[1,4,128,256]{3,2,1,0:T(8,128)(2,1)} %get-tuple-element.54), channel_id=1, source_target_pairs={{0,3},{1,2},{2,1},{3,0},{4,7},{5,6},{6,5},{7,4},{8,11},{9,10},{10,... | collective-permute-start | bytes 786440 | tf_op jit(solution)/shard_map/ppermute | solution.py:67
  17.2 19.0 %collective-permute-start.3 = (bf16[1,4,128,256]{3,2,1,0:T(8,128)(2,1)}, bf16[1,4,128,256]{3,2,1,0:T(8,128)(2,1)}, u32[]{:S(2)}, u32[]{:S(2)}) collective-permute-start(bf16[1,4,128,256]{3,2,1,0:T(8,128)(2,1)} %get-tuple-element.53), channel_id=1, source_target_pairs={{0,4},{1,5},{2,6},{3,7},{4,0},{5,1},{6,2},{7,3},{8,12},{9,13},{10,... | collective-permute-start | bytes 786440 | tf_op jit(solution)/shard_map/ppermute | solution.py:67
  17.7 19.5 %collective-permute-start.4 = (bf16[1,4,128,256]{3,2,1,0:T(8,128)(2,1)}, bf16[1,4,128,256]{3,2,1,0:T(8,128)(2,1)S(1)}, u32[]{:S(2)}, u32[]{:S(2)}) collective-permute-start(bf16[1,4,128,256]{3,2,1,0:T(8,128)(2,1)} %get-tuple-element.52), channel_id=1, source_target_pairs={{0,5},{1,4},{2,7},{3,6},{4,1},{5,0},{6,3},{7,2},{8,13},{9,12},{10,... | collective-permute-start | bytes 786440 | tf_op jit(solution)/shard_map/ppermute | solution.py:67
  22.8 28.4 %all-to-all-start = ((bf16[4,4,128,256]{3,2,1,0:T(8,128)(2,1)}), bf16[4,4,128,256]{3,2,1,0:T(8,128)(2,1)S(1)}, u32[]{:S(2)}, u32[]{:S(2)}) async-start(bf16[4,4,128,256]{3,2,1,0:T(8,128)(2,1)} %broadcast_select_fusion.2), calls=%async_computation | async-start | bytes 2097152 | tf_op jit(solution)/shard_map/all_to_all | solution.py:54
  31.0 10.3 %collective-permute-start.5 = (bf16[1,4,128,256]{3,2,1,0:T(8,128)(2,1)}, bf16[1,4,128,256]{3,2,1,0:T(8,128)(2,1)S(1)}, u32[]{:S(2)}, u32[]{:S(2)}) collective-permute-start(bf16[1,4,128,256]{3,2,1,0:T(8,128)(2,1)} %get-tuple-element.51), channel_id=1, source_target_pairs={{0,6},{1,7},{2,4},{3,5},{4,2},{5,3},{6,0},{7,1},{8,14},{9,15},{10,... | collective-permute-start | bytes 786440 | tf_op jit(solution)/shard_map/ppermute | solution.py:67
  33.5 11.4 %collective-permute-start.6 = (bf16[1,4,128,256]{3,2,1,0:T(8,128)(2,1)}, bf16[1,4,128,256]{3,2,1,0:T(8,128)(2,1)S(1)}, u32[]{:S(2)}, u32[]{:S(2)}) collective-permute-start(bf16[1,4,128,256]{3,2,1,0:T(8,128)(2,1)} %get-tuple-element.50), channel_id=1, source_target_pairs={{0,7},{1,6},{2,5},{3,4},{4,3},{5,2},{6,1},{7,0},{8,15},{9,14},{10,... | collective-permute-start | bytes 786440 | tf_op jit(solution)/shard_map/ppermute | solution.py:67
  44.9 1.4 copy-start.3
  153.5 50.1 %copy-start.7 = (bf16[256,256]{1,0:T(8,128)(2,1)S(1)}, bf16[256,256]{1,0:T(8,128)(2,1)}, u32[]{:S(2)}) copy-start(bf16[256,256]{1,0:T(8,128)(2,1)} %param.30) | copy-start | bytes 393220
  153.5 50.1 %copy-start.8 = (f32[256]{0:T(256)S(1)}, f32[256]{0:T(256)}, u32[]{:S(2)}) copy-start(f32[256]{0:T(256)} %param.31) | copy-start | bytes 3076
  153.5 50.1 %copy-start.9 = (f32[256]{0:T(256)S(1)}, f32[256]{0:T(256)}, u32[]{:S(2)}) copy-start(f32[256]{0:T(256)} %param.29) | copy-start | bytes 3076
  153.6 50.1 %copy-start.10 = (f32[256]{0:T(256)S(1)}, f32[256]{0:T(256)}, u32[]{:S(2)}) copy-start(f32[256]{0:T(256)} %param.28) | copy-start | bytes 3076
